TPU v7x, 32 devices: a whole 2x2x4 slice. The times are simulated.
32 devices in a mesh: group: 2 (over x), row: 8 (over z, y), rhs: 2 (over core).
Axes of the slice: x: 2, y: 2, z: 4, core: 2. Of those that a mesh axis runs over, the one named last changes fastest.
Arguments:
- u_panels: float32 [8192, 1536], P(('group', 'row')), parts along dimension 0, may hold values from -0.078125 to 0.078125
- u_diag: float32 [3072], P('group'), parts along dimension 0, may hold values from 0.5 to 2
- l_panels: float32 [8192, 1536], P(('group', 'row')), parts along dimension 0, may hold values from -0.078125 to 0.078125
- right_side: float32 [8192, 512], P(('group', 'row'), 'rhs'), parts along dimension 0, may hold values from -6 to 6
- x_tail: float32 [8192, 512], P(('group', 'row'), 'rhs'), parts along dimension 0, may hold values from -6 to 6
- slot_blocks: int32 [16], P('group'), parts along dimension 0, may hold values from 0 to 7, as said below
Outputs:
- forward_out: float32 [8192, 512], P(('group', 'row'), 'rhs'), parts along dimension 0
- solution: float32 [8192, 512], P(('group', 'row'), 'rhs'), parts along dimension 0
There are 2 independent parts, one for each index of `group`. A program takes and returns all parts, laid end to end along the dimension named above; each array names one. Nothing has to cross between parts.
Inputs may be any that keep to these rules, and one draw needn't show every extreme that they name: `slot_blocks`: a permutation of the 8 global row blocks, each named once.
All inputs are finite; a program needn't handle non-finite values.
Results may differ from a plain program's by a relative error of at most 0.000065.
Values sent between devices are 32-bit elements; how exact they have to be, the bound alone decides.
A program may use at most 64 MiB of HBM per device.

v0:
```python
import jax
import jax.numpy as jnp
from jax import lax
from jax.sharding import PartitionSpec as P

PANEL = 512
PANELS = 3


def from_root(shard, axis, root):
    mine = lax.axis_index(axis) == root
    return lax.psum(jnp.where(mine, shard, jnp.zeros_like(shard)), axis)


def lower_masked(panels, my_blocks, panel_size):
    count = my_blocks.shape[0]
    within = lax.broadcasted_iota(jnp.int32, (count, panel_size), 1)
    global_row = (my_blocks[:, None] * panel_size + within).reshape(count * panel_size)
    column = lax.broadcasted_iota(jnp.int32, (1, panels.shape[1]), 1)
    return jnp.where(global_row[:, None] > column, panels, 0.0)


def pick_block(stacked, my_blocks, target):
    picked = (my_blocks == target)[:, None, None]
    return jnp.sum(jnp.where(picked, stacked, 0.0), axis=0)


def owner_of(slot_blocks, target, count):
    position = jnp.argmax(slot_blocks == target)
    return position // count


def product(left, right):
    return jnp.dot(left, right, precision=lax.Precision.HIGHEST, preferred_element_type=jnp.float32)


def inner_rows(left, right):
    return lax.dot_general(
        left,
        right,
        (((0,), (0,)), ((), ())),
        precision=lax.Precision.HIGHEST,
        preferred_element_type=jnp.float32,
    )


def body(u_panels, u_diag, l_panels, right_side, x_tail, slot_blocks):
    panel_size = PANEL
    rows_here = u_panels.shape[0]
    count = rows_here // panel_size
    width = right_side.shape[1]
    my_blocks = lax.dynamic_slice_in_dim(slot_blocks, lax.axis_index("row") * count, count)
    upper_low = lower_masked(u_panels, my_blocks, panel_size)
    lower_low = lower_masked(l_panels, my_blocks, panel_size)
    lower_stack = lower_low.reshape(count, panel_size, lower_low.shape[1])
    upper_stack = upper_low.reshape(count, panel_size, upper_low.shape[1])
    tail_rows = (my_blocks >= PANELS)[:, None, None]
    tail_values = jnp.where(tail_rows, x_tail.reshape(count, panel_size, width), 0.0).reshape(
        rows_here, width
    )
    partial_value = inner_rows(lower_low, tail_values)
    state = right_side.reshape(count, panel_size, width)
    solved = []
    for panel_index in range(PANELS):
        start = panel_index * panel_size
        diag_block = pick_block(
            upper_stack[:, :, start : start + panel_size], my_blocks, panel_index
        )
        diag_block = diag_block + jnp.diag(u_diag[start : start + panel_size])
        local_rhs = pick_block(state, my_blocks, panel_index)
        local_values = lax.linalg.triangular_solve(
            diag_block, local_rhs, left_side=True, lower=True
        )
        holder = owner_of(slot_blocks, panel_index, count)
        panel_values = from_root(local_values, "row", holder)
        update = product(upper_low[:, start : start + panel_size], panel_values).reshape(
            count, panel_size, width
        )
        state = jnp.where((my_blocks > panel_index)[:, None, None], state - update, state)
        state = jnp.where((my_blocks == panel_index)[:, None, None], panel_values[None], state)
        solved.append(panel_values)
    forward_out = state.reshape(rows_here, width)
    result = x_tail.reshape(count, panel_size, width)
    for panel_index in reversed(range(PANELS)):
        start = panel_index * panel_size
        summed = lax.psum(partial_value[start : start + panel_size], "row")
        diag_block = pick_block(
            lower_stack[:, :, start : start + panel_size], my_blocks, panel_index
        )
        panel_x = lax.linalg.triangular_solve(
            diag_block,
            solved[panel_index] - summed,
            left_side=True,
            lower=True,
            transpose_a=True,
            unit_diagonal=True,
        )
        result = jnp.where((my_blocks == panel_index)[:, None, None], panel_x[None], result)
        if panel_index > 0:
            own_rows = pick_block(lower_stack[:, :, :start], my_blocks, panel_index)
            partial_value = jnp.concatenate(
                [partial_value[:start] + inner_rows(own_rows, panel_x), partial_value[start:]],
                axis=0,
            )
    solution = result.reshape(rows_here, width)
    return (forward_out, solution)


def solution(mesh):
    placed = (
        P(("group", "row"), None),
        P("group"),
        P(("group", "row"), None),
        P(("group", "row"), "rhs"),
        P(("group", "row"), "rhs"),
        P("group"),
    )
    return jax.shard_map(
        body,
        mesh=mesh,
        in_specs=placed,
        out_specs=(P(("group", "row"), "rhs"), P(("group", "row"), "rhs")),
        check_vma=False,
    )
```

profile of v0, /device:TPU:0, one launch (start us, length us, event | category | flops | bytes accessed | tf_op | source)
XLA Modules:
  0.0 524.5 jit_solution(5620329260580295217)
XLA Ops:
  7.2 1.3 compare_reduce_fusion
  14.0 4.9 fusion.4
  18.9 2.1 fusion.34
  21.0 11.7 %while.12 = (s32[]{:T(128)}, f32[512,512]{1,0:T(8,128)}, s32[4,2]{0,1:T(2,128)S(1)}, f32[4,128,128]{2,1,0:T(8,128)S(1)}, s32[]{:T(128)}) while((s32[]{:T(128)}, f32[512,512]{1,0:T(8,128)}, s32[4,2]{0,1:T(2,128)S(1)}, f32[4,128,128]{2,1,0:T(8,128)S(1)}, s32[]{:T(128)}) %tuple.110), condition=%wide.while_cond, body=%wide.while_body.sunk | while | flops 2 | bytes 131189 | solution.py:71
  21.7 2.3 bitcast_dynamic-update-slice_fusion.12
  24.6 2.3 bitcast_dynamic-update-slice_fusion.12
  27.6 2.3 bitcast_dynamic-update-slice_fusion.12
  30.5 2.2 bitcast_dynamic-update-slice_fusion.12
  33.4 40.1 %custom-call.10 = f32[4,128,128]{1,2,0:T(8,128)S(1)} custom-call(f32[4,128,128]{2,1,0:T(8,128)} %copy-done.19), custom_call_target="InvertDiagBlocksLowerTriangular" | custom-call | tf_op jit(solution)/shard_map/triangular_solve/custom-call.1 | solution.py:71
  80.3 1.4 convolution_subtract_fusion.13
  81.7 1.8 fusion.137
  84.1 1.7 maximum_select_fusion
  86.7 12.0 %while.13 = (s32[]{:T(128)}, f32[512,512]{1,0:T(8,128)}, s32[4,2]{0,1:T(2,128)S(1)}, f32[4,128,128]{2,1,0:T(8,128)S(1)}, s32[]{:T(128)}) while((s32[]{:T(128)}, f32[512,512]{1,0:T(8,128)}, s32[4,2]{0,1:T(2,128)S(1)}, f32[4,128,128]{2,1,0:T(8,128)S(1)}, s32[]{:T(128)}) %tuple.139), condition=%wide.while_cond.clone, body=%wide.while_body.clone.sunk | while | flops 2 | bytes 131189 | solution.py:71
  87.4 2.3 bitcast_dynamic-update-slice_fusion.13
  90.4 2.3 bitcast_dynamic-update-slice_fusion.13
  93.4 2.3 bitcast_dynamic-update-slice_fusion.13
  96.4 2.3 bitcast_dynamic-update-slice_fusion.13
  99.4 40.1 %custom-call.11 = f32[4,128,128]{1,2,0:T(8,128)S(1)} custom-call(f32[4,128,128]{2,1,0:T(8,128)} %copy-done.20), custom_call_target="InvertDiagBlocksLowerTriangular" | custom-call | tf_op jit(solution)/shard_map/triangular_solve/custom-call.1 | solution.py:71
  140.3 14.2 %while.14 = (s32[]{:T(128)}, f32[512,512]{1,0:T(8,128)}, s32[4,2]{0,1:T(2,128)S(1)}, f32[4,128,128]{2,1,0:T(8,128)}, s32[]{:T(128)}) while((s32[]{:T(128)}, f32[512,512]{1,0:T(8,128)}, s32[4,2]{0,1:T(2,128)S(1)}, f32[4,128,128]{2,1,0:T(8,128)}, s32[]{:T(128)}) %tuple.140), condition=%wide.while_cond.clone.1, body=%wide.while_body.clone.1.sunk | while | flops 2 | bytes 132205 | solution.py:71
  140.9 2.9 bitcast_dynamic-update-slice_fusion.14
  144.5 2.9 bitcast_dynamic-update-slice_fusion.14
  148.1 2.9 bitcast_dynamic-update-slice_fusion.14
  151.7 2.8 bitcast_dynamic-update-slice_fusion.14
  156.4 8.3 %fusion.2 = f32[1536,256]{1,0:T(8,128)} fusion(f32[512,1536]{1,0:T(8,128)} %param.12, s32[512]{0:T(512)S(1)} %iota_add_fusion.1, f32[512,256]{1,0:T(8,128)} %param.14, pred[]{:T(512)} %bitcast.26), kind=kOutput, calls=%fused_computation.15 | convolution fusion | flops 2417623040 | bytes 5244929 | tf_op jit(solution)/shard_map/dot_general | solution.py:38
  164.8 3.2 broadcast_select_fusion.1
  171.2 1.3 convolution_subtract_fusion.11
  175.3 40.1 %custom-call.12 = f32[4,128,128]{1,2,0:T(8,128)S(1)} custom-call(f32[4,128,128]{2,1,0:T(8,128)} %get-tuple-element.52), custom_call_target="InvertDiagBlocksLowerTriangular" | custom-call | tf_op jit(solution)/shard_map/triangular_solve/custom-call.1 | solution.py:71
  216.1 1.9 slice.320
  218.0 4.0 convert_add_fusion.2
  222.0 27.3 %all-reduce.9.cloned.1.call-done = f32[512,256]{1,0:T(8,128)} async-done(((f32[512,256]{1,0:T(8,128)}), f32[512,256]{1,0:T(8,128)}) %all-reduce.9.cloned.1.call-update) | async-done | bytes 524304 | tf_op jit(solution)/shard_map/psum | solution.py:12
  249.3 3.2 broadcast_select_fusion
  255.7 1.3 convolution_subtract_fusion.9
  258.2 11.2 %while.15 = (s32[]{:T(128)}, f32[512,512]{1,0:T(8,128)}, s32[4,2]{0,1:T(2,128)S(1)}, f32[4,128,128]{2,1,0:T(8,128)S(1)}, s32[]{:T(128)}) while((s32[]{:T(128)}, f32[512,512]{1,0:T(8,128)}, s32[4,2]{0,1:T(2,128)S(1)}, f32[4,128,128]{2,1,0:T(8,128)S(1)}, s32[]{:T(128)}) %tuple.141), condition=%wide.while_cond.1, body=%wide.while_body.1.sunk | while | flops 2 | bytes 131189 | solution.py:90
  258.9 2.2 bitcast_dynamic-update-slice_fusion.15
  261.7 2.2 bitcast_dynamic-update-slice_fusion.15
  264.5 2.2 bitcast_dynamic-update-slice_fusion.15
  267.3 2.1 bitcast_dynamic-update-slice_fusion.15
  270.1 40.1 %custom-call.13 = f32[4,128,128]{1,2,0:T(8,128)S(1)} custom-call(f32[4,128,128]{2,1,0:T(8,128)} %copy-done.21), custom_call_target="InvertDiagBlocksLowerTriangular" | custom-call | tf_op jit(solution)/shard_map/triangular_solve/custom-call.0 | solution.py:90
  310.3 26.2 %all-reduce.15.cloned.1.call-done = (f32[512,256]{1,0:T(8,128)}, f32[512,256]{1,0:T(8,128)}) async-done(((f32[512,256]{1,0:T(8,128)}, f32[512,256]{1,0:T(8,128)}), (f32[512,256]{1,0:T(8,128)}, f32[512,256]{1,0:T(8,128)})) %all-reduce.15.cloned.1.call-update) | async-done | bytes 1048592 | tf_op jit(solution)/shard_map/psum | solution.py:12
  336.5 1.4 sub.28
  340.5 1.3 convolution_subtract_fusion.8
  342.9 1.5 convolution_subtract_fusion.7
  345.5 3.5 fusion.10
  351.9 13.6 %while.16 = (s32[]{:T(128)}, f32[512,512]{1,0:T(8,128)}, s32[4,2]{0,1:T(2,128)S(1)}, f32[4,128,128]{2,1,0:T(8,128)}, s32[]{:T(128)}) while((s32[]{:T(128)}, f32[512,512]{1,0:T(8,128)}, s32[4,2]{0,1:T(2,128)S(1)}, f32[4,128,128]{2,1,0:T(8,128)}, s32[]{:T(128)}) %tuple.142), condition=%wide.while_cond.1.clone, body=%wide.while_body.1.clone.sunk | while | flops 2 | bytes 132205 | solution.py:90
  352.5 2.8 bitcast_dynamic-update-slice_fusion.16
  355.9 2.8 bitcast_dynamic-update-slice_fusion.16
  359.3 2.8 bitcast_dynamic-update-slice_fusion.16
  362.7 2.7 bitcast_dynamic-update-slice_fusion.16
  365.5 40.7 %custom-call.14 = f32[4,128,128]{1,2,0:T(8,128)} custom-call(f32[4,128,128]{2,1,0:T(8,128)} %get-tuple-element.54), custom_call_target="InvertDiagBlocksLowerTriangular" | custom-call | tf_op jit(solution)/shard_map/triangular_solve/custom-call.0 | solution.py:90
  406.2 17.2 %all-reduce.11.cloned.1.call-done = f32[512,256]{1,0:T(8,128)} async-done(((f32[512,256]{1,0:T(8,128)}), f32[512,256]{1,0:T(8,128)}) %all-reduce.11.cloned.1.call-update) | async-done | bytes 524304 | tf_op jit(solution)/shard_map/psum | solution.py:86
  423.5 1.4 sub.29
  428.2 1.3 convolution_subtract_fusion.6
  429.8 1.5 convolution_subtract_fusion.5
  432.2 3.9 convolution_add_fusion
  436.8 13.6 %while.17 = (s32[]{:T(128)}, f32[512,512]{1,0:T(8,128)}, s32[4,2]{0,1:T(2,128)S(1)}, f32[4,128,128]{2,1,0:T(8,128)}, s32[]{:T(128)}) while((s32[]{:T(128)}, f32[512,512]{1,0:T(8,128)}, s32[4,2]{0,1:T(2,128)S(1)}, f32[4,128,128]{2,1,0:T(8,128)}, s32[]{:T(128)}) %tuple.143), condition=%wide.while_cond.1.clone.1, body=%wide.while_body.1.clone.1.sunk | while | flops 2 | bytes 132205 | solution.py:90
  437.5 2.8 bitcast_dynamic-update-slice_fusion.17
  440.9 2.8 bitcast_dynamic-update-slice_fusion.17
  444.3 2.8 bitcast_dynamic-update-slice_fusion.17
  447.7 2.7 bitcast_dynamic-update-slice_fusion.17
  451.1 40.8 %custom-call.15 = f32[4,128,128]{1,2,0:T(8,128)} custom-call(f32[4,128,128]{2,1,0:T(8,128)} %get-tuple-element.55), custom_call_target="InvertDiagBlocksLowerTriangular" | custom-call | tf_op jit(solution)/shard_map/triangular_solve/custom-call.0 | solution.py:90
  491.8 3.2 fusion.14
  495.1 13.5 %all-reduce.13.cloned.1.call-done = f32[512,256]{1,0:T(8,128)} async-done(((f32[512,256]{1,0:T(8,128)}), f32[512,256]{1,0:T(8,128)}) %all-reduce.13.cloned.1.call-update) | async-done | bytes 524304 | tf_op jit(solution)/shard_map/psum | solution.py:86
  513.3 1.3 convolution_subtract_fusion.4
  514.8 1.4 convolution_subtract_fusion.3
  (157 shorter events, 57.4 us)
Async XLA Ops:
  7.2 157.6 %all-reduce.7.cloned.1.call-start = ((), (), s32[]{:S(2)}) async-start(), calls=%async_computation | async-start | bytes 1048576 | tf_op jit(solution)/shard_map/psum | solution.py:12
  32.7 0.7 copy-start.19
  73.6 0.7 copy-start.18
  76.7 77.8 %copy-start.22 = (s32[8]{0:T(128)S(1)}, s32[8]{0:T(128)}, u32[]{:S(2)}) copy-start(s32[8]{0:T(128)} %param.15) | copy-start | bytes 100
  85.8 163.4 %all-reduce.9.cloned.1.call-start = ((), (), s32[]{:S(2)}) async-start(), calls=%async_computation.1 | async-start | bytes 1048576 | tf_op jit(solution)/shard_map/psum | solution.py:12
  98.7 0.7 copy-start.20
  173.7 162.8 %all-reduce.15.cloned.1.call-start = ((), (), s32[]{:S(2)}) async-start(), calls=%async_computation.4 | async-start | bytes 2097152 | tf_op jit(solution)/shard_map/psum | solution.py:12
  258.1 165.3 %all-reduce.11.cloned.1.call-start = ((), (), s32[]{:S(2)}) async-start(), calls=%async_computation.2 | async-start | bytes 1048576 | tf_op jit(solution)/shard_map/psum | solution.py:86
  269.4 0.7 copy-start.21
  310.3 27.6 %copy-start.16 = (f32[4,128,128]{1,2,0:T(8,128)}, f32[4,128,128]{1,2,0:T(8,128)S(1)}, u32[]{:S(2)}) copy-start(f32[4,128,128]{1,2,0:T(8,128)S(1)} %custom-call.13) | copy-start | bytes 786436
  336.5 9.0 %copy-start = (f32[1,512,1536]{2,1,0:T(8,128)S(1)}, f32[1,512,1536]{2,1,0:T(8,128)}, u32[]{:S(2)}) copy-start(f32[1,512,1536]{2,1,0:T(8,128)} %get-tuple-element.127) | copy-start | bytes 9437188
  336.5 9.0 %copy-start.1 = (f32[1536,256]{1,0:T(8,128)S(1)}, f32[1536,256]{1,0:T(8,128)}, u32[]{:S(2)}) copy-start(f32[1536,256]{1,0:T(8,128)} %fusion.2) | copy-start | bytes 4718596
  342.9 6.1 %copy-start.7 = (f32[128,256]{1,0:T(8,128)}, f32[128,256]{1,0:T(8,128)S(1)}, u32[]{:S(2)}) copy-start(f32[128,256]{1,0:T(8,128)S(1)} %fusion.126) | copy-start | bytes 393220
  345.5 3.5 copy-start.11
  349.0 1.0 copy-start.2
  350.9 157.8 %all-reduce.13.cloned.1.call-start = ((), (), s32[]{:S(2)}) async-start(), calls=%async_computation.3 | async-start | bytes 1048576 | tf_op jit(solution)/shard_map/psum | solution.py:86
  423.4 6.1 %copy-start.17 = (f32[4,128,128]{1,2,0:T(8,128)S(1)}, f32[4,128,128]{1,2,0:T(8,128)}, u32[]{:S(2)}) copy-start(f32[4,128,128]{1,2,0:T(8,128)} %custom-call.14) | copy-start | bytes 786436
  423.5 8.8 %copy-start.3 = (f32[1024,256]{1,0:T(8,128)S(1)}, f32[1024,256]{1,0:T(8,128)}, u32[]{:S(2)}) copy-start(f32[1024,256]{1,0:T(8,128)} %copy-done.2) | copy-start | bytes 3145732
  428.2 3.4 copy-start.4
  429.8 1.8 copy-start.9
  431.6 0.6 copy-start.13
  495.1 19.5 %copy-start.15 = (f32[4,128,128]{1,2,0:T(8,128)S(1)}, f32[4,128,128]{1,2,0:T(8,128)}, u32[]{:S(2)}) copy-start(f32[4,128,128]{1,2,0:T(8,128)} %custom-call.15) | copy-start | bytes 786436
  495.1 21.5 %copy-start.5 = (f32[128,256]{1,0:T(8,128)S(1)}, f32[128,256]{1,0:T(8,128)}, u32[]{:S(2)}) copy-start(f32[128,256]{1,0:T(8,128)} %copy-done.4) | copy-start | bytes 393220
  495.1 21.5 %copy-start.6 = (f32[512,256]{1,0:T(8,128)S(1)}, f32[512,256]{1,0:T(8,128)}, u32[]{:S(2)}) copy-start(f32[512,256]{1,0:T(8,128)} %param.14) | copy-start | bytes 1572868
  495.1 21.5 %copy-start.8 = (f32[128,256]{1,0:T(8,128)S(1)}, f32[128,256]{1,0:T(8,128)}, u32[]{:S(2)}) copy-start(f32[128,256]{1,0:T(8,128)} %copy-done.7) | copy-start | bytes 393220
  495.1 21.5 %copy-start.10 = (f32[128,256]{1,0:T(8,128)S(1)}, f32[128,256]{1,0:T(8,128)}, u32[]{:S(2)}) copy-start(f32[128,256]{1,0:T(8,128)} %copy-done.9) | copy-start | bytes 393220
  495.1 21.5 %copy-start.12 = (f32[128,256]{1,0:T(8,128)S(1)}, f32[128,256]{1,0:T(8,128)}, u32[]{:S(2)}) copy-start(f32[128,256]{1,0:T(8,128)} %copy-done.11) | copy-start | bytes 393220
  495.1 21.5 %copy-start.14 = (f32[128,256]{1,0:T(8,128)S(1)}, f32[128,256]{1,0:T(8,128)}, u32[]{:S(2)}) copy-start(f32[128,256]{1,0:T(8,128)} %copy-done.13) | copy-start | bytes 393220
Sparse Core Ops, SparseCore 0:
  86.0 75.5 all-reduce.6
  173.8 75.3 all-reduce.8
  258.3 78.1 all-reduce.14
  351.0 72.4 all-reduce.10
  436.2 72.3 all-reduce.12
where the time goes:
time: 532 us; the launch traced here: 525 us
  other arithmetic  265 us (50%)
  local copies, waits for them, and re-layouts  87.4 us (16%)
  waiting for transfers between devices  84.3 us (16%)
  matrix products  64.8 us (12%)
  between operations  21.9 us (4%)
    another operation x5, other arithmetic, body(): lax.linalg.triangular_solve(diag_block, solved[panel_index] - summed, lef...  126 us
    another operation x5, other arithmetic, body(): lax.linalg.triangular_solve(diag_block, local_rhs, left_side=True, lower=...  122 us
    psum x3, waiting for transfers between devices, from_root(): return lax.psum(jnp.where(mine, shard, jnp.zeros_like(shard)), axis)  53.5 us
    another operation x43, local copies, waits for them, and re-layouts, body(): lax.linalg.triangular_solve(diag_block, local_rhs, left_side=True, lower=...  40 us
    another operation x36, local copies, waits for them, and re-layouts, body(): lax.linalg.triangular_solve(diag_block, solved[panel_index] - summed, lef...  38.3 us
    psum x2, waiting for transfers between devices, body(): summed = lax.psum(partial_value[start:start + panel_size], 'row')  30.8 us
    another operation x21, matrix products, body(): lax.linalg.triangular_solve(diag_block, solved[panel_index] - summed, lef...  20.8 us
    another operation x21, matrix products, body(): lax.linalg.triangular_solve(diag_block, local_rhs, left_side=True, lower=...  18.8 us
  transfers between devices with their start and end apart: 5, of which 4 were waited for; matrix products, arithmetic and copies ran while one was open for 55% of the time, Pallas kernels for 0%

commit v1 on v0

v1 whole, which is shorter than its diff:
```python
import functools

import jax
import jax.numpy as jnp
from jax import lax
from jax.experimental import pallas as pl
from jax.experimental.pallas import tpu as pltpu
from jax.sharding import PartitionSpec as P

PANEL = 512
PANELS = 3
TILE = 128
BASE = 16
F32 = jnp.float32
NN = (((1,), (0,)), ((), ()))
TN = (((0,), (0,)), ((), ()))


def split(value):
    high = value.astype(jnp.bfloat16)
    return high, (value - high.astype(F32)).astype(jnp.bfloat16)


def dot3(left, right, dims=NN):
    lh, ll = split(left)
    rh, rl = split(right)
    dot = functools.partial(lax.dot_general, dimension_numbers=dims, preferred_element_type=F32)
    return dot(lh, rh) + (dot(lh, rl) + dot(ll, rh))


def unit_inverse(strict):
    size = strict.shape[0]
    row = lax.broadcasted_iota(jnp.int32, (TILE, TILE), 0)
    col = lax.broadcasted_iota(jnp.int32, (TILE, TILE), 1)
    eye = jnp.where(row == col, 1.0, 0.0)
    done = []
    for start in range(0, size, TILE):
        tile = strict[start : start + TILE, start : start + TILE]
        power = jnp.where(row // BASE == col // BASE, tile, 0.0)
        inverse = eye - power
        order = 2
        while order < BASE:
            power = dot3(power, power)
            inverse = inverse + dot3(inverse, power)
            order *= 2
        block = BASE
        while block < TILE:
            off = jnp.where(
                (row // (2 * block) == col // (2 * block)) & (row // block != col // block), tile, 0.0
            )
            inverse = inverse - dot3(inverse, dot3(off, inverse))
            block *= 2
        done.append(inverse)
    block = TILE
    while block < size:
        merged = []
        for index in range(0, len(done), 2):
            start = index * block
            off = strict[start + block : start + 2 * block, start : start + block]
            corner = -dot3(done[index + 1], dot3(off, done[index]))
            top = jnp.concatenate([done[index], jnp.zeros_like(corner)], axis=1)
            merged.append(jnp.concatenate([top, jnp.concatenate([corner, done[index + 1]], axis=1)], axis=0))
        done = merged
        block *= 2
    return done[0]


def strictly_lower(block):
    row = lax.broadcasted_iota(jnp.int32, block.shape, 0)
    col = lax.broadcasted_iota(jnp.int32, block.shape, 1)
    return jnp.where(row > col, block, 0.0)


def upper_start(place, panel, diag, rhs, inverse, first):
    mine = place[1]
    inverse[...] = jnp.zeros_like(inverse)
    first[...] = jnp.zeros_like(first)

    @pl.when(mine < PANELS)
    def _():
        row = lax.broadcasted_iota(jnp.int32, (TILE, TILE), 0)
        col = lax.broadcasted_iota(jnp.int32, (TILE, TILE), 1)
        across = diag[0]
        down = jnp.concatenate(
            [
                jnp.sum(
                    jnp.where(row == col, across[:, start : start + TILE], 0.0), axis=1, keepdims=True
                )
                for start in range(0, PANEL, TILE)
            ],
            axis=0,
        )
        strict = strictly_lower(panel[...]) / down
        inverse[...] = unit_inverse(strict) / across

    @pl.when(mine == 0)
    def _():
        first[...] = dot3(inverse[...], rhs[...])


def lower_start(place, diag_panel, panel, tail, inverse, partial):
    mine = place[1]

    @pl.when(mine < PANELS)
    def _():
        inverse[...] = unit_inverse(strictly_lower(diag_panel[...])).T
        partial[...] = jnp.zeros_like(partial)

    @pl.when(mine >= PANELS)
    def _():
        inverse[...] = jnp.zeros_like(inverse)
        partial[...] = dot3(panel[...], tail[...], TN)


def tail_product(place, panel, tail, partial):
    mine = place[1]
    partial[...] = jnp.zeros_like(partial)

    @pl.when(mine >= PANELS)
    def _():
        partial[...] = dot3(panel[...], tail[...], TN)


def forward_step(index, place, panel, inverse, values, state, after, candidate):
    mine = place[1]
    after[...] = state[...]

    @pl.when(mine > index)
    def _():
        after[...] = state[...] - dot3(panel[...], values[...])

    @pl.when(mine == index)
    def _():
        after[...] = values[...]

    candidate[...] = jnp.zeros_like(candidate)

    @pl.when(mine == index + 1)
    def _():
        candidate[...] = dot3(inverse[...], after[...])


def last_forward(place, panel, inverse, values, state, lower_inverse, below, partial, summed, after, candidate, solved, sent):
    mine = place[1]
    last = PANELS - 1
    after[...] = state[...]
    candidate[...] = jnp.zeros_like(candidate)
    solved[...] = jnp.zeros_like(solved)
    sent[...] = partial[...]

    @pl.when(mine > last - 1)
    def _():
        after[...] = state[...] - dot3(panel[...], values[...])

    @pl.when(mine == last - 1)
    def _():
        after[...] = values[...]

    @pl.when(mine == last)
    def _():
        candidate[...] = dot3(inverse[...], after[...])
        solved[...] = dot3(lower_inverse[...], candidate[...] - summed[...])
        sent[...] = dot3(below[...], solved[...], TN)


def backward_step(index, place, inverse, forward, summed, partial, result, below, solved, sent):
    mine = place[1]
    solved[...] = result[...]
    sent[...] = partial[...]

    @pl.when(mine == index)
    def _():
        solved[...] = dot3(inverse[...], forward[...] - summed[...])
        sent[...] = dot3(below[...], solved[...], TN)


def backward_last(place, inverse, forward, summed, result, tail, solved):
    mine = place[1]
    solved[...] = result[...]

    @pl.when(mine == 0)
    def _():
        solved[...] = dot3(inverse[...], forward[...] - summed[...])

    @pl.when(mine >= PANELS)
    def _():
        solved[...] = tail[...]


def forward_end(place, panel, values, state, after):
    mine = place[1]
    after[...] = state[...]

    @pl.when(mine >= PANELS)
    def _():
        after[...] = state[...] - dot3(panel[...], values[...])

    @pl.when(mine == PANELS - 1)
    def _():
        after[...] = values[...]


def full(shape):
    return pl.BlockSpec(shape, lambda step, place: (0,) * len(shape))


def columns(index, width=1):
    return pl.BlockSpec((PANEL, width * PANEL), lambda step, place: (0, index))


OWN = pl.BlockSpec((PANEL, PANEL), lambda step, place: (0, place[0]))


def call(kernel, place, ins, outs):
    arrays = [array for array, _ in ins]
    specs = [full(array.shape) if spec is None else spec for array, spec in ins]
    return pl.pallas_call(
        kernel,
        grid_spec=pltpu.PrefetchScalarGridSpec(
            num_scalar_prefetch=1,
            grid=(1,),
            in_specs=specs,
            out_specs=[full(shape) for shape in outs],
        ),
        out_shape=[jax.ShapeDtypeStruct(shape, F32) for shape in outs],
        compiler_params=pltpu.CompilerParams(vmem_limit_bytes=40 * 1024 * 1024),
    )(place, *arrays)


def body(u_panels, u_diag, l_panels, right_side, x_tail, slot_blocks):
    width = right_side.shape[1]
    mine = slot_blocks[lax.axis_index("row")]
    place = jnp.stack([jnp.minimum(mine, PANELS - 1), mine]).astype(jnp.int32)
    square, block = (PANEL, PANEL), (PANEL, width)
    diag = u_diag.reshape(PANELS, 1, PANEL)
    last = PANELS - 1
    total = lambda value: lax.psum(value, "row")

    (part2,) = call(tail_product, place, [(l_panels, columns(last)), (x_tail, None)], [block])
    sum2 = total(part2)
    upper_inv, first = call(
        upper_start,
        place,
        [
            (u_panels, OWN),
            (diag, pl.BlockSpec((1, 1, PANEL), lambda step, place: (place[0], 0, 0))),
            (right_side, None),
        ],
        [square, block],
    )
    y0 = total(first)
    lower_inv, part01 = call(
        lower_start,
        place,
        [(l_panels, OWN), (l_panels, columns(0, last)), (x_tail, None)],
        [square, (last * PANEL, width)],
    )
    state, second = call(
        functools.partial(forward_step, 0),
        place,
        [(u_panels, columns(0)), (upper_inv, None), (y0, None), (right_side, None)],
        [block, block],
    )
    y1 = total(second)
    state, third, result, sent = call(
        last_forward,
        place,
        [
            (u_panels, columns(1)),
            (upper_inv, None),
            (y1, None),
            (state, None),
            (lower_inv, None),
            (l_panels, columns(0, last)),
            (part01, None),
            (sum2, None),
        ],
        [block, block, block, (last * PANEL, width)],
    )
    sum1 = total(sent[PANEL:])
    third, sum1 = lax.optimization_barrier((third, sum1))
    result, sent0 = call(
        functools.partial(backward_step, 1),
        place,
        [
            (lower_inv, None),
            (y1, None),
            (sum1, None),
            (sent[:PANEL], None),
            (result, None),
            (l_panels, columns(0)),
        ],
        [block, block],
    )
    sum0 = total(sent0)
    y2 = total(third)
    (forward_out,) = call(
        forward_end, place, [(u_panels, columns(last)), (y2, None), (state, None)], [block]
    )
    (solution_out,) = call(
        backward_last,
        place,
        [(lower_inv, None), (y0, None), (sum0, None), (result, None), (x_tail, None)],
        [block],
    )
    return (forward_out, solution_out)


def solution(mesh):
    placed = (
        P(("group", "row"), None),
        P("group"),
        P(("group", "row"), None),
        P(("group", "row"), "rhs"),
        P(("group", "row"), "rhs"),
        P("group"),
    )
    return jax.shard_map(
        body,
        mesh=mesh,
        in_specs=placed,
        out_specs=(P(("group", "row"), "rhs"), P(("group", "row"), "rhs")),
        check_vma=False,
    )
```

time: 532 us -> 372 us (0.70); the launches traced: 525 us -> 370 us
  other arithmetic: 265 us -> 0.72 us
  waiting for transfers between devices: 84.3 us -> 290 us
  matrix products: 64.8 us -> 0 us
  local copies, waits for them, and re-layouts: 87.4 us -> 41.6 us
  Pallas kernels: 0 us -> 22.3 us
  between operations: 21.9 us -> 14.6 us
    another operation x13 -> x1, other arithmetic: 251 us -> 0.72 us  [body(): place = jnp.stack([jnp.minimum(mine, PANELS - 1), mine]).astype(jnp.int32)]
    psum x5 -> x4, waiting for transfers between devices: 84.3 us -> 290 us  [body(): total = lambda value: lax.psum(value, 'row')]
    another operation x79 -> x0, local copies, waits for them, and re-layouts: 78.2 us -> none  [the longest x43 40 us: body(): lax.linalg.triangular_solve(diag_block, local_rhs, left_side=True, lower=...]
    another operation x42 -> x0, matrix products: 39.6 us -> none  [the longest x21 20.8 us: body(): lax.linalg.triangular_solve(diag_block, solved[panel_index] - summed, lef...]
    unnamed x46 -> x82, local copies, waits for them, and re-layouts: 4.48 us -> 38.4 us
    dot_general x6 -> x0, matrix products: 25.2 us -> none  [the longest x3 15.7 us: inner_rows(): lax.dot_general(left, right, (((0,), (0,)), ((), ())), precision=lax.Prec...]
    pallas_call x0 -> x8, Pallas kernels: none -> 22.3 us  [call(): pl.pallas_call(kernel, grid_spec=pltpu.PrefetchScalarGridSpec(num_scalar_...]
  transfers between devices with their start and end apart: 5 -> 4, of which waited for: 4 -> 4; matrix products, arithmetic and copies ran while one was open for 55% -> 0% of each run, Pallas kernels for 0% -> 2%
where the time goes in v1:
time: 372 us; the launch traced here: 370 us
  waiting for transfers between devices  290 us (78%)
  local copies, waits for them, and re-layouts  41.6 us (11%)
  Pallas kernels  22.3 us (6%)
  between operations  14.6 us (4%)
    psum x4, waiting for transfers between devices, body(): total = lambda value: lax.psum(value, 'row')  290 us
    unnamed x82, local copies, waits for them, and re-layouts  38.4 us
    pallas_call x8, Pallas kernels, call(): pl.pallas_call(kernel, grid_spec=pltpu.PrefetchScalarGridSpec(num_scalar_...  22.3 us
  transfers between devices with their start and end apart: 4, of which 4 were waited for; matrix products, arithmetic and copies ran while one was open for 0% of the time, Pallas kernels for 2%

profile of v1, /device:TPU:0, one launch (start us, length us, event | category | flops | bytes accessed | tf_op | source)
XLA Modules:
  0.0 369.9 jit_solution(14174320830025755659)
XLA Ops:
  7.2 0.0 all-reduce.7.cloned.1.call-start
  7.2 1.4 dynamic_slice.3
  9.3 0.7 pad_add_fusion.place
  10.0 0.7 reshape.10.diag
  10.7 1.9 copy-done.1
  12.6 1.0 copy-done.19
  13.6 8.2 %shard_map.77 = (f32[512,512]{1,0:T(8,128)S(1)}, f32[512,256]{1,0:T(8,128)S(1)}) custom-call(s32[2]{0:T(128)S(1)} %pad_add_fusion.place, f32[512,1536]{1,0:T(8,128)S(1)} %copy-done.1, f32[3,1,512]{2,1,0:T(1,128)S(1)} %reshape.10.diag, f32[512,256]{1,0:T(8,128)S(1)} %copy-done.19), custom_call_target="tpu_custom_call" | custom-call | tf_op jit(solution)/shard_map/pallas_call | solution.py:217
  21.9 1.0 copy-done.12
  22.8 0.8 copy-done.37
  23.6 0.0 all-reduce.7.cloned.1.call-update
  23.7 0.0 all-reduce.13.cloned.1.call-start
  23.7 0.0 copy-start.9
  23.7 1.0 copy-done.9
  24.8 0.6 shard_map.80
  25.4 0.8 copy-done.17
  26.2 70.2 %all-reduce.7.cloned.1.call-done.values.forward = f32[512,256]{1,0:T(8,128)} async-done(((f32[512,256]{1,0:T(8,128)}), f32[512,256]{1,0:T(8,128)}) %all-reduce.7.cloned.1.call-update) | async-done | bytes 524304 | tf_op jit(solution)/shard_map/psum | solution.py:237
  96.4 1.9 copy-done.2
  98.3 1.2 copy-done.13
  99.5 1.0 copy-done.20
  100.5 1.0 copy-done.21
  101.6 0.7 shard_map.78
  102.3 0.8 copy-done.27
  103.1 0.8 copy-done.35
  103.9 0.0 all-reduce.13.cloned.1.call-update
  103.9 0.0 all-reduce.9.cloned.1.call-start
  104.0 0.0 copy-start.10
  104.0 1.0 copy-done.10
  105.0 7.6 %shard_map.79 = (f32[512,512]{1,0:T(8,128)S(1)}, f32[1024,256]{1,0:T(8,128)S(1)}) custom-call(s32[2]{0:T(128)S(1)} %pad_add_fusion.place, f32[512,1536]{1,0:T(8,128)S(1)} %copy-done, f32[512,1536]{1,0:T(8,128)S(1)} %copy-done, f32[512,256]{1,0:T(8,128)S(1)} %copy-done.10), custom_call_target="tpu_custom_call" | custom-call | tf_op jit(solution)/shard_map/pallas_call | solution.py:217
  112.6 1.0 copy-done.5
  113.6 1.0 copy-done.23
  114.6 67.8 %all-reduce.13.cloned.1.call-done = (f32[512,256]{1,0:T(8,128)}, f32[512,256]{1,0:T(8,128)}) async-done(((f32[512,256]{1,0:T(8,128)}, f32[512,256]{1,0:T(8,128)}), (f32[512,256]{1,0:T(8,128)}, f32[512,256]{1,0:T(8,128)})) %all-reduce.13.cloned.1.call-update) | async-done | bytes 1048592 | tf_op jit(solution)/shard_map/psum | solution.py:237
  182.4 1.9 copy-done.3
  184.3 1.2 copy-done.6
  185.5 1.2 copy-done.14
  186.7 1.0 copy-done.15
  187.8 1.2 copy-done.24
  189.0 1.0 copy-done.28
  190.0 1.0 copy-done.31
  191.1 1.1 shard_map.81
  192.2 0.0 copy-start.34
  192.2 1.1 fusion
  193.4 0.1 copy-done.29
  193.5 0.2 copy-done.34
  193.7 0.0 all-reduce.9.cloned.1.call-update
  193.7 0.0 all-reduce.11.cloned.1.call-start
  193.7 73.8 %all-reduce.9.cloned.1.call-done.summed = f32[512,256]{1,0:T(8,128)} async-done(((f32[512,256]{1,0:T(8,128)}), f32[512,256]{1,0:T(8,128)}) %all-reduce.9.cloned.1.call-update) | async-done | bytes 524304 | tf_op jit(solution)/shard_map/psum | solution.py:237
  267.6 1.2 copy-done.7
  268.8 1.0 copy-done.16
  269.8 1.0 copy-done.18
  270.9 1.0 copy-done.30
  271.9 1.0 copy-done.32
  273.0 0.7 shard_map.83
  273.6 0.0 copy-start.36
  273.7 0.8 copy-done.36
  274.4 0.8 copy-done.38
  275.2 0.0 all-reduce.11.cloned.1.call-update
  275.3 78.6 %all-reduce.11.cloned.1.call-done = (f32[512,256]{1,0:T(8,128)}, f32[512,256]{1,0:T(8,128)}) async-done(((f32[512,256]{1,0:T(8,128)}, f32[512,256]{1,0:T(8,128)}), (f32[512,256]{1,0:T(8,128)}, f32[512,256]{1,0:T(8,128)})) %all-reduce.11.cloned.1.call-update) | async-done | bytes 1048592 | tf_op jit(solution)/shard_map/psum | solution.py:237
  353.8 1.9 copy-done.4
  355.7 1.0 copy-done.26
  356.8 1.0 copy-done.33
  357.8 1.4 shard_map.82
  359.3 1.0 copy-done.11
  360.3 1.0 copy-done.22
  361.3 2.0 shard_map.84
  (42 shorter events, 0.1 us)
Async XLA Ops:
  7.2 16.5 %copy-start = (f32[512,1536]{1,0:T(8,128)S(1)}, f32[512,1536]{1,0:T(8,128)}, u32[]{:S(2)}) copy-start(f32[512,1536]{1,0:T(8,128)} %below.3) | copy-start | bytes 9437188
  7.2 89.2 %all-reduce.7.cloned.1.call-start = ((), (), s32[]{:S(2)}) async-start(), calls=%async_computation | async-start | bytes 1048576 | tf_op jit(solution)/shard_map/psum | solution.py:237
  10.7 1.9 copy-start.1
  12.6 1.0 copy-start.19
  21.9 1.0 copy-start.12
  22.8 0.8 copy-start.37
  23.7 158.7 %all-reduce.13.cloned.1.call-start = ((), (), s32[]{:S(2)}) async-start(), calls=%async_computation.3 | async-start | bytes 2097152 | tf_op jit(solution)/shard_map/psum | solution.py:237
  23.7 1.0 copy-start.9
  25.4 0.8 copy-start.17
  96.4 1.9 copy-start.2
  98.3 1.2 copy-start.13
  99.5 1.0 copy-start.20
  100.5 1.0 copy-start.21
  102.3 0.8 copy-start.27
  103.1 0.8 copy-start.35
  103.9 163.6 %all-reduce.9.cloned.1.call-start = ((), (), s32[]{:S(2)}) async-start(), calls=%async_computation.1 | async-start | bytes 1048576 | tf_op jit(solution)/shard_map/psum | solution.py:237
  104.0 1.0 copy-start.10
  112.6 1.0 copy-start.5
  113.6 1.0 copy-start.23
  182.4 1.9 copy-start.3
  184.3 1.2 copy-start.6
  185.5 1.2 copy-start.14
  186.7 1.0 copy-start.15
  187.8 1.2 copy-start.24
  189.0 1.0 copy-start.28
  190.0 1.0 copy-start.31
  192.2 1.2 copy-start.25
  192.2 1.3 copy-start.29
  192.2 1.5 copy-start.34
  193.7 160.1 %all-reduce.11.cloned.1.call-start = ((), (), s32[]{:S(2)}) async-start(), calls=%async_computation.2 | async-start | bytes 2097152 | tf_op jit(solution)/shard_map/psum | solution.py:237
  267.6 1.2 copy-start.7
  268.8 1.0 copy-start.16
  269.8 1.0 copy-start.18
  270.9 1.0 copy-start.30
  271.9 1.0 copy-start.32
  273.6 0.8 copy-start.36
  274.4 0.8 copy-start.38
  275.2 84.0 %copy-start.8 = (f32[512,512]{1,0:T(8,128)S(1)}, f32[512,512]{1,0:T(8,128)}, u32[]{:S(2)}) copy-start(f32[512,512]{1,0:T(8,128)} %copy-done.5) | copy-start | bytes 3145732
  353.8 1.9 copy-start.4
  355.7 1.0 copy-start.26
  356.8 1.0 copy-start.33
  357.8 1.4 copy-start.39
  357.8 1.4 copy-start.40
  359.3 1.0 copy-start.11
  360.3 1.0 copy-start.22
Sparse Core Ops, SparseCore 0:
  23.8 72.5 all-reduce.6
  104.1 78.2 all-reduce.12
  193.8 73.7 all-reduce.8
  275.4 78.3 all-reduce.10

commit v2 on v1

v2 whole, which is shorter than its diff:
```python
import functools

import jax
import jax.numpy as jnp
from jax import lax
from jax.experimental import pallas as pl
from jax.experimental.pallas import tpu as pltpu
from jax.sharding import PartitionSpec as P

PANEL = 512
PANELS = 3
TILE = 128
BASE = 16
F32 = jnp.float32
NN = (((1,), (0,)), ((), ()))
TN = (((0,), (0,)), ((), ()))


def split(value):
    high = value.astype(jnp.bfloat16)
    return high, (value - high.astype(F32)).astype(jnp.bfloat16)


def dot3(left, right, dims=NN):
    lh, ll = split(left)
    rh, rl = split(right)
    dot = functools.partial(lax.dot_general, dimension_numbers=dims, preferred_element_type=F32)
    return dot(lh, rh) + (dot(lh, rl) + dot(ll, rh))


def unit_inverse(strict):
    size = strict.shape[0]
    row = lax.broadcasted_iota(jnp.int32, (TILE, TILE), 0)
    col = lax.broadcasted_iota(jnp.int32, (TILE, TILE), 1)
    eye = jnp.where(row == col, 1.0, 0.0)
    done = []
    for start in range(0, size, TILE):
        tile = strict[start : start + TILE, start : start + TILE]
        power = jnp.where(row // BASE == col // BASE, tile, 0.0)
        inverse = eye - power
        order = 2
        while order < BASE:
            power = dot3(power, power)
            inverse = inverse + dot3(inverse, power)
            order *= 2
        block = BASE
        while block < TILE:
            off = jnp.where(
                (row // (2 * block) == col // (2 * block)) & (row // block != col // block), tile, 0.0
            )
            inverse = inverse - dot3(inverse, dot3(off, inverse))
            block *= 2
        done.append(inverse)
    block = TILE
    while block < size:
        merged = []
        for index in range(0, len(done), 2):
            start = index * block
            off = strict[start + block : start + 2 * block, start : start + block]
            corner = -dot3(done[index + 1], dot3(off, done[index]))
            top = jnp.concatenate([done[index], jnp.zeros_like(corner)], axis=1)
            merged.append(jnp.concatenate([top, jnp.concatenate([corner, done[index + 1]], axis=1)], axis=0))
        done = merged
        block *= 2
    return done[0]


def strictly_lower(block):
    row = lax.broadcasted_iota(jnp.int32, block.shape, 0)
    col = lax.broadcasted_iota(jnp.int32, block.shape, 1)
    return jnp.where(row > col, block, 0.0)


def prepare(place, u_own, l_own, diag, rhs, lower, tail, upper_inv, lower_inv, first, partial):
    mine = place[1]
    first[...] = jnp.zeros_like(first)

    @pl.when(mine < PANELS)
    def _():
        row = lax.broadcasted_iota(jnp.int32, (TILE, TILE), 0)
        col = lax.broadcasted_iota(jnp.int32, (TILE, TILE), 1)
        across = diag[0]
        down = jnp.concatenate(
            [
                jnp.sum(
                    jnp.where(row == col, across[:, start : start + TILE], 0.0), axis=1, keepdims=True
                )
                for start in range(0, PANEL, TILE)
            ],
            axis=0,
        )
        upper_inv[...] = unit_inverse(strictly_lower(u_own[...]) / down) / across
        lower_inv[...] = unit_inverse(strictly_lower(l_own[...])).T
        partial[...] = jnp.zeros_like(partial)

    @pl.when(mine == 0)
    def _():
        first[...] = dot3(upper_inv[...], rhs[...])

    @pl.when(mine >= PANELS)
    def _():
        upper_inv[...] = jnp.zeros_like(upper_inv)
        lower_inv[...] = jnp.zeros_like(lower_inv)
        partial[...] = dot3(lower[...], tail[...], TN).reshape(partial.shape)


class Sum:
    def __init__(self, index, source, pair_in, held, line_in, result, sends, recvs):
        self.source, self.result = source, result
        self.pair_in, self.held, self.line_in = pair_in.at[index], held.at[index], line_in.at[index]
        self.sends, self.recvs = sends.at[index], recvs.at[index]
        self.outer = lax.axis_size("row") // 2
        self.slice = PANEL // (2 * self.outer)
        me = lax.axis_index("row")
        self.side, self.along = me % 2, me // 2
        self.partner = self.along * 2 + 1 - self.side
        self.started = []

    def rows(self, side, along):
        start = side * (PANEL // 2) + along * self.slice
        return pl.ds(pl.multiple_of(start, self.slice), self.slice)

    def peer(self, offset):
        return lax.rem(self.along + offset, self.outer)

    def before(self, offset):
        return lax.rem(self.along + self.outer - offset, self.outer)

    def send(self, stage, slot, source, target, device):
        copy = pltpu.make_async_remote_copy(
            src_ref=source,
            dst_ref=target,
            send_sem=self.sends.at[stage, slot],
            recv_sem=self.recvs.at[stage, slot],
            device_id={"row": device},
            device_id_type=pl.DeviceIdType.MESH,
        )
        copy.start()
        self.started.append(copy)
        return copy

    def order(self):
        return list(range(1, self.outer)) + [0]

    def start(self):
        self.pair = {}
        for offset in self.order():
            rows = self.rows(1 - self.side, self.peer(offset))
            self.pair[offset] = self.send(
                0, offset, self.source.at[rows], self.pair_in.at[offset], self.partner
            )

    def middle(self):
        self.line = {}
        for offset in self.order():
            self.pair[offset].wait_recv()
            rows = self.rows(self.side, self.peer(offset))
            self.held[offset] = self.source[rows, :] + self.pair_in[offset]
            if offset:
                self.line[offset] = self.send(
                    1,
                    offset,
                    self.held.at[offset],
                    self.line_in.at[offset],
                    self.peer(offset) * 2 + self.side,
                )

    def finish(self):
        whole = self.held[0]
        for offset in range(1, self.outer):
            self.line[offset].wait_recv()
            whole = whole + self.line_in[offset]
        rows = self.rows(self.side, self.along)
        self.result[rows, :] = whole
        self.back = {}
        self.last = {}
        part = self.result.at[rows]
        for offset in range(1, self.outer):
            self.back[offset] = self.send(
                2, offset, part, part, self.peer(offset) * 2 + self.side
            )
        self.last[0] = self.send(3, 0, part, part, self.partner)

    def gather(self):
        for offset in range(1, self.outer):
            self.back[offset].wait_recv()
            part = self.result.at[self.rows(self.side, self.before(offset))]
            self.last[offset] = self.send(3, offset, part, part, self.partner)

    def end(self):
        for offset in range(self.outer):
            self.last[offset].wait_recv()

    def drain(self):
        for copy in self.started:
            copy.wait_send()


def chain(
    place, upper, lower, upper_inv, lower_inv, rhs, tail, first, partial,
    forward_out, solution_out,
    y0, y1, y2, s0, s1, s2, state, held_x, c1, c2, c3, c4, pair_in, held, line_in, sends, recvs,
):
    outer = lax.axis_size("row") // 2
    me = lax.axis_index("row")
    side, along = me % 2, me // 2
    barrier = pltpu.get_barrier_semaphore()
    peers = [along * 2 + 1 - side]
    peers += [lax.rem(along + offset, outer) * 2 + side for offset in range(1, outer)]
    for peer in peers:
        pl.semaphore_signal(
            barrier, inc=1, device_id={"row": peer}, device_id_type=pl.DeviceIdType.MESH
        )
    pl.semaphore_wait(barrier, len(peers))

    mine = jnp.full(rhs.shape, place[1], jnp.int32)

    def make(index, source, result):
        return Sum(index, source, pair_in, held, line_in, result, sends, recvs)

    sum_y0 = make(0, first, y0)
    sum_c2 = make(1, partial.at[2], s2)
    sum_y0.start()
    sum_c2.start()
    sum_y0.middle()
    sum_c2.middle()
    sum_y0.finish()
    sum_y0.gather()
    sum_c2.finish()
    sum_y0.end()

    state[...] = rhs[...] - jnp.where(mine > 0, dot3(upper[:, :PANEL], y0[...]), 0.0)
    c1[...] = jnp.where(mine == 1, dot3(upper_inv[...], state[...]), 0.0)
    sum_y1 = make(2, c1, y1)
    sum_y1.start()
    sum_c2.gather()
    sum_y1.middle()
    sum_y1.finish()
    sum_y1.gather()
    sum_c2.end()
    sum_y1.end()

    state[...] = state[...] - jnp.where(mine > 1, dot3(upper[:, PANEL : 2 * PANEL], y1[...]), 0.0)
    c2[...] = jnp.where(mine == 2, dot3(upper_inv[...], state[...]), 0.0)
    held_x[...] = jnp.where(mine == 2, dot3(lower_inv[...], c2[...] - s2[...]), 0.0)
    c3[...] = partial[1] + dot3(lower[:, PANEL : 2 * PANEL], held_x[...], TN)
    sum_c1 = make(3, c3, s1)
    sum_y2 = make(4, c2, y2)
    sum_c1.start()
    sum_y2.start()
    c4[...] = partial[0] + dot3(lower[:, :PANEL], held_x[...], TN)
    sum_c1.middle()
    sum_y2.middle()
    sum_c1.finish()
    sum_c1.gather()
    sum_y2.finish()
    sum_c1.end()

    x1 = jnp.where(mine == 1, dot3(lower_inv[...], y1[...] - s1[...]), 0.0)
    held_x[...] = held_x[...] + x1
    c4[...] = c4[...] + dot3(lower[:, :PANEL], x1, TN)
    sum_c0 = make(5, c4, s0)
    sum_c0.start()
    sum_y2.gather()
    sum_c0.middle()
    sum_y2.end()
    sum_c0.finish()
    sum_c0.gather()
    past = state[...] - dot3(upper[:, 2 * PANEL :], y2[...])
    own = jnp.where(mine == 0, y0[...], jnp.where(mine == 1, y1[...], y2[...]))
    forward_out[...] = jnp.where(mine >= PANELS, past, own)
    sum_c0.end()
    x0 = dot3(lower_inv[...], y0[...] - s0[...])
    head = jnp.where(mine == 0, x0, held_x[...])
    solution_out[...] = jnp.where(mine >= PANELS, tail[...], head)
    for one in (sum_y0, sum_c2, sum_y1, sum_c1, sum_y2, sum_c0):
        one.drain()


def full(shape):
    return pl.BlockSpec(shape, lambda step, place: (0,) * len(shape))


OWN = pl.BlockSpec((PANEL, PANEL), lambda step, place: (0, place[0]))


def body(row_count, u_panels, u_diag, l_panels, right_side, x_tail, slot_blocks):
    width = right_side.shape[1]
    mine = slot_blocks[lax.axis_index("row")]
    place = jnp.stack([jnp.minimum(mine, PANELS - 1), mine]).astype(jnp.int32)
    square, block = (PANEL, PANEL), (PANEL, width)
    diag = u_diag.reshape(PANELS, 1, PANEL)
    limit = pltpu.CompilerParams(vmem_limit_bytes=40 * 1024 * 1024)
    shapes = [square, square, block, (PANELS, *block)]
    upper_inv, lower_inv, first, partial = pl.pallas_call(
        prepare,
        grid_spec=pltpu.PrefetchScalarGridSpec(
            num_scalar_prefetch=1,
            grid=(1,),
            in_specs=[
                OWN,
                OWN,
                pl.BlockSpec((1, 1, PANEL), lambda step, place: (place[0], 0, 0)),
                full(block),
                full(l_panels.shape),
                full(block),
            ],
            out_specs=[full(shape) for shape in shapes],
        ),
        out_shape=[jax.ShapeDtypeStruct(shape, F32) for shape in shapes],
        compiler_params=limit,
    )(place, u_panels, l_panels, diag, right_side, l_panels, x_tail)
    outer = row_count // 2
    piece = PANEL // row_count
    sums = 6
    vmem = pl.BlockSpec(memory_space=pltpu.VMEM)
    slots = pltpu.VMEM((sums, outer, piece, width), F32)
    return pl.pallas_call(
        chain,
        in_specs=[pl.BlockSpec(memory_space=pltpu.SMEM)] + [vmem] * 8,
        out_specs=[vmem] * 2,
        out_shape=[jax.ShapeDtypeStruct(block, F32)] * 2,
        scratch_shapes=[pltpu.VMEM(block, F32)] * 12
        + [slots] * 3
        + [pltpu.SemaphoreType.DMA((sums, 4, outer))] * 2,
        compiler_params=pltpu.CompilerParams(
            collective_id=0, has_side_effects=True, vmem_limit_bytes=48 * 1024 * 1024
        ),
    )(place, u_panels, l_panels, upper_inv, lower_inv, right_side, x_tail, first, partial)


def solution(mesh):
    placed = (
        P(("group", "row"), None),
        P("group"),
        P(("group", "row"), None),
        P(("group", "row"), "rhs"),
        P(("group", "row"), "rhs"),
        P("group"),
    )
    return jax.shard_map(
        functools.partial(body, mesh.shape["row"]),
        mesh=mesh,
        in_specs=placed,
        out_specs=(P(("group", "row"), "rhs"), P(("group", "row"), "rhs")),
        check_vma=False,
    )
```

time: 372 us -> 136 us (0.37)
  waiting for transfers between devices: 290 us -> 0 us
  Pallas kernels: 22.3 us -> 123 us
  local copies, waits for them, and re-layouts: 41.6 us -> 10.5 us
  between operations: 14.6 us -> 1.32 us
    psum x4 -> x0, waiting for transfers between devices: 290 us -> none  [body(): total = lambda value: lax.psum(value, 'row')]
    pallas_call x8 -> x2, Pallas kernels: 22.3 us -> 123 us  [the longest x1 121 us: body(): pl.pallas_call(chain, in_specs=[pl.BlockSpec(memory_space=pltpu.SMEM)] +...]
    unnamed x82 -> x16, local copies, waits for them, and re-layouts: 38.4 us -> 8.6 us
  transfers between devices with their start and end apart: 4 -> 0, of which waited for: 4 -> 0; matrix products, arithmetic and copies ran while one was open for 0% -> 0% of each run, Pallas kernels for 2% -> 0%
where the time goes in v2:
time: 136 us
  Pallas kernels  123 us (90%)
  local copies, waits for them, and re-layouts  10.5 us (8%)
    pallas_call x1, Pallas kernels, body(): pl.pallas_call(chain, in_specs=[pl.BlockSpec(memory_space=pltpu.SMEM)] +...  121 us
    unnamed x16, local copies, waits for them, and re-layouts  8.6 us

profile of v2, /device:TPU:0, one launch (start us, length us, event | category | flops | bytes accessed | tf_op | source)
XLA Modules:
  0.0 135.8 jit_solution(4327874188832983125)
XLA Ops:
  0.6 1.2 dynamic_slice.3
  2.5 0.7 pad_add_fusion.place
  3.2 0.7 reshape.10.diag
  4.0 0.0 copy-start
  4.0 1.9 %copy-done = f32[512,1536]{1,0:T(8,128)S(1)} copy-done((f32[512,1536]{1,0:T(8,128)S(1)}, f32[512,1536]{1,0:T(8,128)}, u32[]{:S(2)}) %copy-start) | copy-done | bytes 3145752
  5.8 0.0 copy-start.1
  5.8 1.9 %copy-done.1 = f32[512,1536]{1,0:T(8,128)S(1)} copy-done((f32[512,1536]{1,0:T(8,128)S(1)}, f32[512,1536]{1,0:T(8,128)}, u32[]{:S(2)}) %copy-start.1) | copy-done | bytes 3145752
  7.7 0.0 copy-start.2
  7.7 1.0 copy-done.2
  8.8 0.0 copy-start.4
  8.8 1.0 copy-done.4
  9.8 0.0 copy-start.3
  9.8 0.0 copy-start.5
  9.8 2.5 %shard_map.77 = (f32[512,512]{1,0:T(8,128)S(1)}, f32[512,512]{1,0:T(8,128)S(1)}, f32[512,256]{1,0:T(8,128)S(1)}, f32[3,512,256]{2,1,0:T(8,128)S(1)}) custom-call(s32[2]{0:T(128)S(1)} %pad_add_fusion.place, f32[512,1536]{1,0:T(8,128)S(1)} %copy-done.1, f32[512,1536]{1,0:T(8,128)S(1)} %copy-done, f32[3,1,512]{2,1,0:T(1,128)S(1)} %reshape.10.diag, ...), custom_call_target="tpu_custom_call" | custom-call | tf_op jit(solution)/shard_map/pallas_call | solution.py:295
  12.3 0.0 copy-start.6
  12.3 1.1 copy-done.6
  13.4 0.0 copy-done.3
  13.4 0.0 copy-done.5
  13.4 120.7 %shard_map.78 = (f32[512,256]{1,0:T(8,128)S(1)}, f32[512,256]{1,0:T(8,128)S(1)}) custom-call(s32[2]{0:T(128)S(1)} %pad_add_fusion.place, f32[512,1536]{1,0:T(8,128)} %upper.1, f32[512,1536]{1,0:T(8,128)} %lower.3, f32[512,512]{1,0:T(8,128)S(1)} %get-tuple-element.6.upper_inv, f32[512,512]{1,0:T(8,128)S(1)} %get-tuple-element.7.lower_inv, ...), custom_call_target="tpu_custom_call" | custom-call | tf_op jit(solution)/shard_map/pallas_call | solution.py:318
  134.2 0.8 copy.10
  135.0 0.8 copy.11
Async XLA Ops:
  4.0 1.9 %copy-start = (f32[512,1536]{1,0:T(8,128)S(1)}, f32[512,1536]{1,0:T(8,128)}, u32[]{:S(2)}) copy-start(f32[512,1536]{1,0:T(8,128)} %lower.3) | copy-start | bytes 9437188
  5.8 1.9 %copy-start.1 = (f32[512,1536]{1,0:T(8,128)S(1)}, f32[512,1536]{1,0:T(8,128)}, u32[]{:S(2)}) copy-start(f32[512,1536]{1,0:T(8,128)} %upper.1) | copy-start | bytes 9437188
  7.7 1.0 copy-start.2
  8.8 1.0 copy-start.4
  9.8 3.6 %copy-start.3 = (f32[512,256]{1,0:T(8,128)S(1)}, f32[512,256]{1,0:T(8,128)}, u32[]{:S(2)}) copy-start(f32[512,256]{1,0:T(8,128)} %rhs.3) | copy-start | bytes 1572868
  9.8 3.6 %copy-start.5 = (f32[512,256]{1,0:T(8,128)S(1)}, f32[512,256]{1,0:T(8,128)}, u32[]{:S(2)}) copy-start(f32[512,256]{1,0:T(8,128)} %tail.3) | copy-start | bytes 1572868
  12.3 1.1 copy-start.6

commit v3 on v2

--- a/solution.py
+++ b/solution.py
@@ -28,15 +28,14 @@
     return dot(lh, rh) + (dot(lh, rl) + dot(ll, rh))
 
 
-def unit_inverse(strict):
-    size = strict.shape[0]
+def inverse_stages(part, size):
     row = lax.broadcasted_iota(jnp.int32, (TILE, TILE), 0)
     col = lax.broadcasted_iota(jnp.int32, (TILE, TILE), 1)
     eye = jnp.where(row == col, 1.0, 0.0)
     done = []
     for start in range(0, size, TILE):
-        tile = strict[start : start + TILE, start : start + TILE]
-        power = jnp.where(row // BASE == col // BASE, tile, 0.0)
+        tile = part(start, start, TILE)
+        power = jnp.where((row // BASE == col // BASE) & (row > col), tile, 0.0)
         inverse = eye - power
         order = 2
         while order < BASE:
@@ -46,62 +45,25 @@
         block = BASE
         while block < TILE:
             off = jnp.where(
-                (row // (2 * block) == col // (2 * block)) & (row // block != col // block), tile, 0.0
+                (row // (2 * block) == col // (2 * block)) & (row // block > col // block), tile, 0.0
             )
             inverse = inverse - dot3(inverse, dot3(off, inverse))
             block *= 2
         done.append(inverse)
+        if start % (2 * TILE):
+            yield None
     block = TILE
     while block < size:
         merged = []
         for index in range(0, len(done), 2):
             start = index * block
-            off = strict[start + block : start + 2 * block, start : start + block]
+            off = part(start + block, start, block)
             corner = -dot3(done[index + 1], dot3(off, done[index]))
             top = jnp.concatenate([done[index], jnp.zeros_like(corner)], axis=1)
             merged.append(jnp.concatenate([top, jnp.concatenate([corner, done[index + 1]], axis=1)], axis=0))
         done = merged
         block *= 2
-    return done[0]
-
-
-def strictly_lower(block):
-    row = lax.broadcasted_iota(jnp.int32, block.shape, 0)
-    col = lax.broadcasted_iota(jnp.int32, block.shape, 1)
-    return jnp.where(row > col, block, 0.0)
-
-
-def prepare(place, u_own, l_own, diag, rhs, lower, tail, upper_inv, lower_inv, first, partial):
-    mine = place[1]
-    first[...] = jnp.zeros_like(first)
-
-    @pl.when(mine < PANELS)
-    def _():
-        row = lax.broadcasted_iota(jnp.int32, (TILE, TILE), 0)
-        col = lax.broadcasted_iota(jnp.int32, (TILE, TILE), 1)
-        across = diag[0]
-        down = jnp.concatenate(
-            [
-                jnp.sum(
-                    jnp.where(row == col, across[:, start : start + TILE], 0.0), axis=1, keepdims=True
-                )
-                for start in range(0, PANEL, TILE)
-            ],
-            axis=0,
-        )
-        upper_inv[...] = unit_inverse(strictly_lower(u_own[...]) / down) / across
-        lower_inv[...] = unit_inverse(strictly_lower(l_own[...])).T
-        partial[...] = jnp.zeros_like(partial)
-
-    @pl.when(mine == 0)
-    def _():
-        first[...] = dot3(upper_inv[...], rhs[...])
-
-    @pl.when(mine >= PANELS)
-    def _():
-        upper_inv[...] = jnp.zeros_like(upper_inv)
-        lower_inv[...] = jnp.zeros_like(lower_inv)
-        partial[...] = dot3(lower[...], tail[...], TN).reshape(partial.shape)
+    yield done[0]
 
 
 class Sum:
@@ -197,13 +159,28 @@
 
 
 def chain(
-    place, upper, lower, upper_inv, lower_inv, rhs, tail, first, partial,
+    slots, upper_far, lower_far, diag, rhs_far, tail_far,
     forward_out, solution_out,
-    y0, y1, y2, s0, s1, s2, state, held_x, c1, c2, c3, c4, pair_in, held, line_in, sends, recvs,
+    upper, lower, rhs, tail, own, upper_inv, lower_inv, first, part2,
+    y0, y1, y2, s0, s1, s2, state, held_x, c1, c2, c3, c4, pair_in, held, line_in, sends, recvs, loads,
 ):
     outer = lax.axis_size("row") // 2
     me = lax.axis_index("row")
     side, along = me % 2, me // 2
+
+    def load(index, source, target):
+        copy = pltpu.make_async_copy(source, target, loads.at[index])
+        copy.start()
+        return copy
+
+    cols = [pl.ds(index * PANEL, PANEL) for index in range(PANELS)]
+    got_tail = load(0, tail_far, tail)
+    got_lower = {2: load(1, lower_far.at[:, cols[2]], lower.at[2])}
+    got_upper = [load(2 + index, upper_far.at[:, cols[index]], upper.at[index]) for index in range(PANELS)]
+    got_rhs = load(5, rhs_far, rhs)
+    got_lower[0] = load(6, lower_far.at[:, cols[0]], lower.at[0])
+    got_lower[1] = load(7, lower_far.at[:, cols[1]], lower.at[1])
+
     barrier = pltpu.get_barrier_semaphore()
     peers = [along * 2 + 1 - side]
     peers += [lax.rem(along + offset, outer) * 2 + side for offset in range(1, outer)]
@@ -213,42 +190,84 @@
         )
     pl.semaphore_wait(barrier, len(peers))
 
-    mine = jnp.full(rhs.shape, place[1], jnp.int32)
+    block_id = slots[me]
+    mine = jnp.full(rhs.shape, block_id, jnp.int32)
+    mine_square = jnp.full((PANEL, PANEL), block_id, jnp.int32)
+    mine_across = jnp.full((1, PANEL), block_id, jnp.int32)
+
+    def choose(which, values):
+        return jnp.where(which == 0, values[0], jnp.where(which == 1, values[1], values[2]))
+
+    def partial(index):
+        return dot3(lower[index], jnp.where(mine >= PANELS, tail[...], 0.0), TN)
 
     def make(index, source, result):
         return Sum(index, source, pair_in, held, line_in, result, sends, recvs)
 
+    got_tail.wait()
+    got_lower[2].wait()
+    part2[...] = partial(2)
+    sum_c2 = make(1, part2, s2)
+    sum_c2.start()
+
+    for copy in got_upper:
+        copy.wait()
+    across = choose(mine_across, [diag[:, index * PANEL : (index + 1) * PANEL] for index in range(PANELS)])
+    row = lax.broadcasted_iota(jnp.int32, (TILE, TILE), 0)
+    col = lax.broadcasted_iota(jnp.int32, (TILE, TILE), 1)
+    down = [
+        jnp.sum(jnp.where(row == col, across[:, start : start + TILE], 0.0), axis=1, keepdims=True)
+        for start in range(0, PANEL, TILE)
+    ]
+    own[...] = choose(mine_square, upper) / jnp.concatenate(down, axis=0)
+
+    def part(start, first_col, size):
+        return own[start : start + size, first_col : first_col + size]
+
+    stages = inverse_stages(part, PANEL)
+    next(stages)
+    sum_c2.middle()
+    next(stages)
+    upper_inv[...] = next(stages) / across
+    got_rhs.wait()
+    first[...] = jnp.where(mine == 0, dot3(upper_inv[...], rhs[...]), 0.0)
     sum_y0 = make(0, first, y0)
-    sum_c2 = make(1, partial.at[2], s2)
     sum_y0.start()
-    sum_c2.start()
+    got_lower[0].wait()
+    got_lower[1].wait()
+    own[...] = choose(mine_square, lower)
+    stages = inverse_stages(part, PANEL)
+    sum_c2.finish()
+    next(stages)
     sum_y0.middle()
-    sum_c2.middle()
+    sum_c2.gather()
+    next(stages)
     sum_y0.finish()
     sum_y0.gather()
-    sum_c2.finish()
+    lower_inv[...] = next(stages).T
+    sum_c2.end()
     sum_y0.end()
 
-    state[...] = rhs[...] - jnp.where(mine > 0, dot3(upper[:, :PANEL], y0[...]), 0.0)
+    state[...] = rhs[...] - jnp.where(mine > 0, dot3(upper[0], y0[...]), 0.0)
     c1[...] = jnp.where(mine == 1, dot3(upper_inv[...], state[...]), 0.0)
     sum_y1 = make(2, c1, y1)
     sum_y1.start()
-    sum_c2.gather()
+    c3[...] = partial(1)
     sum_y1.middle()
+    c4[...] = partial(0)
     sum_y1.finish()
     sum_y1.gather()
-    sum_c2.end()
     sum_y1.end()
 
-    state[...] = state[...] - jnp.where(mine > 1, dot3(upper[:, PANEL : 2 * PANEL], y1[...]), 0.0)
+    state[...] = state[...] - jnp.where(mine > 1, dot3(upper[1], y1[...]), 0.0)
     c2[...] = jnp.where(mine == 2, dot3(upper_inv[...], state[...]), 0.0)
     held_x[...] = jnp.where(mine == 2, dot3(lower_inv[...], c2[...] - s2[...]), 0.0)
-    c3[...] = partial[1] + dot3(lower[:, PANEL : 2 * PANEL], held_x[...], TN)
+    c3[...] = c3[...] + dot3(lower[1], held_x[...], TN)
     sum_c1 = make(3, c3, s1)
     sum_y2 = make(4, c2, y2)
     sum_c1.start()
     sum_y2.start()
-    c4[...] = partial[0] + dot3(lower[:, :PANEL], held_x[...], TN)
+    c4[...] = c4[...] + dot3(lower[0], held_x[...], TN)
     sum_c1.middle()
     sum_y2.middle()
     sum_c1.finish()
@@ -258,7 +277,7 @@
 
     x1 = jnp.where(mine == 1, dot3(lower_inv[...], y1[...] - s1[...]), 0.0)
     held_x[...] = held_x[...] + x1
-    c4[...] = c4[...] + dot3(lower[:, :PANEL], x1, TN)
+    c4[...] = c4[...] + dot3(lower[0], x1, TN)
     sum_c0 = make(5, c4, s0)
     sum_c0.start()
     sum_y2.gather()
@@ -266,9 +285,8 @@
     sum_y2.end()
     sum_c0.finish()
     sum_c0.gather()
-    past = state[...] - dot3(upper[:, 2 * PANEL :], y2[...])
-    own = jnp.where(mine == 0, y0[...], jnp.where(mine == 1, y1[...], y2[...]))
-    forward_out[...] = jnp.where(mine >= PANELS, past, own)
+    past = state[...] - dot3(upper[2], y2[...])
+    forward_out[...] = jnp.where(mine >= PANELS, past, choose(mine, [y0[...], y1[...], y2[...]]))
     sum_c0.end()
     x0 = dot3(lower_inv[...], y0[...] - s0[...])
     head = jnp.where(mine == 0, x0, held_x[...])
@@ -277,56 +295,31 @@
         one.drain()
 
 
-def full(shape):
-    return pl.BlockSpec(shape, lambda step, place: (0,) * len(shape))
-
-
-OWN = pl.BlockSpec((PANEL, PANEL), lambda step, place: (0, place[0]))
-
-
 def body(row_count, u_panels, u_diag, l_panels, right_side, x_tail, slot_blocks):
     width = right_side.shape[1]
-    mine = slot_blocks[lax.axis_index("row")]
-    place = jnp.stack([jnp.minimum(mine, PANELS - 1), mine]).astype(jnp.int32)
     square, block = (PANEL, PANEL), (PANEL, width)
-    diag = u_diag.reshape(PANELS, 1, PANEL)
-    limit = pltpu.CompilerParams(vmem_limit_bytes=40 * 1024 * 1024)
-    shapes = [square, square, block, (PANELS, *block)]
-    upper_inv, lower_inv, first, partial = pl.pallas_call(
-        prepare,
-        grid_spec=pltpu.PrefetchScalarGridSpec(
-            num_scalar_prefetch=1,
-            grid=(1,),
-            in_specs=[
-                OWN,
-                OWN,
-                pl.BlockSpec((1, 1, PANEL), lambda step, place: (place[0], 0, 0)),
-                full(block),
-                full(l_panels.shape),
-                full(block),
-            ],
-            out_specs=[full(shape) for shape in shapes],
-        ),
-        out_shape=[jax.ShapeDtypeStruct(shape, F32) for shape in shapes],
-        compiler_params=limit,
-    )(place, u_panels, l_panels, diag, right_side, l_panels, x_tail)
     outer = row_count // 2
     piece = PANEL // row_count
     sums = 6
     vmem = pl.BlockSpec(memory_space=pltpu.VMEM)
+    far = pl.BlockSpec(memory_space=pl.ANY)
     slots = pltpu.VMEM((sums, outer, piece, width), F32)
     return pl.pallas_call(
         chain,
-        in_specs=[pl.BlockSpec(memory_space=pltpu.SMEM)] + [vmem] * 8,
+        in_specs=[pl.BlockSpec(memory_space=pltpu.SMEM), far, far, vmem, far, far],
         out_specs=[vmem] * 2,
         out_shape=[jax.ShapeDtypeStruct(block, F32)] * 2,
-        scratch_shapes=[pltpu.VMEM(block, F32)] * 12
+        scratch_shapes=[pltpu.VMEM((PANELS, *square), F32)] * 2
+        + [pltpu.VMEM(block, F32)] * 2
+        + [pltpu.VMEM(square, F32)] * 3
+        + [pltpu.VMEM(block, F32)] * 14
         + [slots] * 3
-        + [pltpu.SemaphoreType.DMA((sums, 4, outer))] * 2,
+        + [pltpu.SemaphoreType.DMA((sums, 4, outer))] * 2
+        + [pltpu.SemaphoreType.DMA((8,))],
         compiler_params=pltpu.CompilerParams(
-            collective_id=0, has_side_effects=True, vmem_limit_bytes=48 * 1024 * 1024
+            collective_id=0, has_side_effects=True, vmem_limit_bytes=56 * 1024 * 1024
         ),
-    )(place, u_panels, l_panels, upper_inv, lower_inv, right_side, x_tail, first, partial)
+    )(slot_blocks, u_panels, l_panels, u_diag.reshape(1, -1), right_side, x_tail)
 
 
 def solution(mesh):

time: 136 us -> 125 us (0.919)
  local copies, waits for them, and re-layouts: 10.5 us -> 5.03 us
  Pallas kernels: 123 us -> 118 us
    pallas_call x2 -> x1, Pallas kernels: 123 us -> 118 us  [body(): pl.pallas_call(chain, in_specs=[pl.BlockSpec(memory_space=pltpu.SMEM), fa...]
    unnamed x16 -> x2, local copies, waits for them, and re-layouts: 8.6 us -> 3.74 us
where the time goes in v3:
time: 125 us; the launch traced here: 124 us
  Pallas kernels  118 us (94%)
  local copies, waits for them, and re-layouts  5.03 us (4%)
    pallas_call x1, Pallas kernels, body(): pl.pallas_call(chain, in_specs=[pl.BlockSpec(memory_space=pltpu.SMEM), fa...  118 us
    unnamed x2, local copies, waits for them, and re-layouts  3.74 us

profile of v3, /device:TPU:0, one launch (start us, length us, event | category | flops | bytes accessed | tf_op | source)
XLA Modules:
  0.0 123.9 jit_solution(6684495930010517519)
XLA Ops:
  0.6 1.3 %reshape.7.diag = f32[1,1536]{1,0:T(1,128)} reshape(f32[1536]{0:T(1024)} %param.7) | data formatting | bytes 12288 | tf_op jit(solution)/shard_map/reshape | solution.py:322
  1.9 118.3 %shard_map.77 = (f32[512,256]{1,0:T(8,128)}, f32[512,256]{1,0:T(8,128)}) custom-call(s32[8]{0:T(128)} %slots.1, f32[512,1536]{1,0:T(8,128)} %upper_far.1, f32[512,1536]{1,0:T(8,128)} %lower_far.1, f32[1,1536]{1,0:T(1,128)} %reshape.7.diag, f32[512,256]{1,0:T(8,128)} %rhs_far.1, f32[512,256]{1,0:T(8,128)} %tail_far.1), custom_call_target="tpu_custom_call" | custom-call | tf_op jit(solution)/shard_map/pallas_call | solution.py:307
  120.2 1.9 %copy.10 = f32[512,256]{1,0:T(8,128)} copy(f32[512,256]{1,0:T(8,128)} %get-tuple-element.4) | data formatting | bytes 1048576
  122.1 1.9 %copy.11 = f32[512,256]{1,0:T(8,128)} copy(f32[512,256]{1,0:T(8,128)} %get-tuple-element.5) | data formatting | bytes 1048576

commit v4 on v3

--- a/solution.py
+++ b/solution.py
@@ -10,6 +10,7 @@
 PANEL = 512
 PANELS = 3
 TILE = 128
+HALVES = 2
 BASE = 16
 F32 = jnp.float32
 NN = (((1,), (0,)), ((), ()))
@@ -25,7 +26,11 @@
     lh, ll = split(left)
     rh, rl = split(right)
     dot = functools.partial(lax.dot_general, dimension_numbers=dims, preferred_element_type=F32)
-    return dot(lh, rh) + (dot(lh, rl) + dot(ll, rh))
+    wide = right.shape[1]
+    if wide > TILE:
+        return dot(lh, rh) + (dot(lh, rl) + dot(ll, rh))
+    both = dot(lh, jnp.concatenate([rh, rl], axis=1))
+    return both[:, :wide] + (both[:, wide:] + dot(ll, rh))
 
 
 def inverse_stages(part, size):
@@ -191,24 +196,34 @@
     pl.semaphore_wait(barrier, len(peers))
 
     block_id = slots[me]
-    mine = jnp.full(rhs.shape, block_id, jnp.int32)
+    half = y0.shape[-1]
+    mine = jnp.full((PANEL, half), block_id, jnp.int32)
     mine_square = jnp.full((PANEL, PANEL), block_id, jnp.int32)
     mine_across = jnp.full((1, PANEL), block_id, jnp.int32)
+    parts = [slice(index * half, (index + 1) * half) for index in range(HALVES)]
 
     def choose(which, values):
         return jnp.where(which == 0, values[0], jnp.where(which == 1, values[1], values[2]))
 
-    def partial(index):
-        return dot3(lower[index], jnp.where(mine >= PANELS, tail[...], 0.0), TN)
+    def partial(index, target):
+        for here, cut in enumerate(parts):
+            target[here] = dot3(lower[index], jnp.where(mine >= PANELS, tail[:, cut], 0.0), TN)
 
     def make(index, source, result):
-        return Sum(index, source, pair_in, held, line_in, result, sends, recvs)
+        return [
+            Sum(
+                index * HALVES + here, source.at[here], pair_in, held, line_in, result.at[here], sends, recvs
+            )
+            for here in range(HALVES)
+        ]
 
     got_tail.wait()
     got_lower[2].wait()
-    part2[...] = partial(2)
-    sum_c2 = make(1, part2, s2)
-    sum_c2.start()
+    partial(2, part2)
+    sum_y0, sum_c2, sum_y1 = make(0, first, y0), make(1, part2, s2), make(2, c1, y1)
+    sum_c1, sum_y2, sum_c0 = make(3, c3, s1), make(4, c2, y2), make(5, c4, s0)
+    for one in sum_c2:
+        one.start()
 
     for copy in got_upper:
         copy.wait()
@@ -226,73 +241,112 @@
 
     stages = inverse_stages(part, PANEL)
     next(stages)
-    sum_c2.middle()
+    for one in sum_c2:
+        one.middle()
     next(stages)
     upper_inv[...] = next(stages) / across
     got_rhs.wait()
-    first[...] = jnp.where(mine == 0, dot3(upper_inv[...], rhs[...]), 0.0)
-    sum_y0 = make(0, first, y0)
-    sum_y0.start()
+    for here, cut in enumerate(parts):
+        first[here] = jnp.where(mine == 0, dot3(upper_inv[...], rhs[:, cut]), 0.0)
+        sum_y0[here].start()
     got_lower[0].wait()
     got_lower[1].wait()
     own[...] = choose(mine_square, lower)
     stages = inverse_stages(part, PANEL)
-    sum_c2.finish()
+    sum_c2[0].finish()
+    sum_y0[0].middle()
+    sum_c2[1].finish()
     next(stages)
-    sum_y0.middle()
-    sum_c2.gather()
+    sum_y0[1].middle()
+    sum_y0[0].finish()
+    sum_y0[0].gather()
     next(stages)
-    sum_y0.finish()
-    sum_y0.gather()
+    sum_y0[1].finish()
+    sum_c2[0].gather()
+    sum_c2[1].gather()
     lower_inv[...] = next(stages).T
-    sum_c2.end()
-    sum_y0.end()
-
-    state[...] = rhs[...] - jnp.where(mine > 0, dot3(upper[0], y0[...]), 0.0)
-    c1[...] = jnp.where(mine == 1, dot3(upper_inv[...], state[...]), 0.0)
-    sum_y1 = make(2, c1, y1)
-    sum_y1.start()
-    c3[...] = partial(1)
-    sum_y1.middle()
-    c4[...] = partial(0)
-    sum_y1.finish()
-    sum_y1.gather()
-    sum_y1.end()
-
-    state[...] = state[...] - jnp.where(mine > 1, dot3(upper[1], y1[...]), 0.0)
-    c2[...] = jnp.where(mine == 2, dot3(upper_inv[...], state[...]), 0.0)
-    held_x[...] = jnp.where(mine == 2, dot3(lower_inv[...], c2[...] - s2[...]), 0.0)
-    c3[...] = c3[...] + dot3(lower[1], held_x[...], TN)
-    sum_c1 = make(3, c3, s1)
-    sum_y2 = make(4, c2, y2)
-    sum_c1.start()
-    sum_y2.start()
-    c4[...] = c4[...] + dot3(lower[0], held_x[...], TN)
-    sum_c1.middle()
-    sum_y2.middle()
-    sum_c1.finish()
-    sum_c1.gather()
-    sum_y2.finish()
-    sum_c1.end()
-
-    x1 = jnp.where(mine == 1, dot3(lower_inv[...], y1[...] - s1[...]), 0.0)
-    held_x[...] = held_x[...] + x1
-    c4[...] = c4[...] + dot3(lower[0], x1, TN)
-    sum_c0 = make(5, c4, s0)
-    sum_c0.start()
-    sum_y2.gather()
-    sum_c0.middle()
-    sum_y2.end()
-    sum_c0.finish()
-    sum_c0.gather()
-    past = state[...] - dot3(upper[2], y2[...])
-    forward_out[...] = jnp.where(mine >= PANELS, past, choose(mine, [y0[...], y1[...], y2[...]]))
-    sum_c0.end()
-    x0 = dot3(lower_inv[...], y0[...] - s0[...])
-    head = jnp.where(mine == 0, x0, held_x[...])
-    solution_out[...] = jnp.where(mine >= PANELS, tail[...], head)
-    for one in (sum_y0, sum_c2, sum_y1, sum_c1, sum_y2, sum_c0):
-        one.drain()
+    sum_y0[0].end()
+
+    def second(here):
+        state[here] = rhs[:, parts[here]] - jnp.where(mine > 0, dot3(upper[0], y0[here]), 0.0)
+        c1[here] = jnp.where(mine == 1, dot3(upper_inv[...], state[here]), 0.0)
+        sum_y1[here].start()
+
+    def third(here):
+        state[here] = state[here] - jnp.where(mine > 1, dot3(upper[1], y1[here]), 0.0)
+        c2[here] = jnp.where(mine == 2, dot3(upper_inv[...], state[here]), 0.0)
+        held_x[here] = jnp.where(mine == 2, dot3(lower_inv[...], c2[here] - s2[here]), 0.0)
+        c3[here] = c3[here] + dot3(lower[1], held_x[here], TN)
+        sum_c1[here].start()
+        sum_y2[here].start()
+        c4[here] = c4[here] + dot3(lower[0], held_x[here], TN)
+
+    def fourth(here):
+        x1 = jnp.where(mine == 1, dot3(lower_inv[...], y1[here] - s1[here]), 0.0)
+        held_x[here] = held_x[here] + x1
+        c4[here] = c4[here] + dot3(lower[0], x1, TN)
+        sum_c0[here].start()
+
+    def forward_end(here):
+        sum_y2[here].end()
+        past = state[here] - dot3(upper[2], y2[here])
+        forward_out[:, parts[here]] = jnp.where(
+            mine >= PANELS, past, choose(mine, [y0[here], y1[here], y2[here]])
+        )
+
+    def backward_end(here):
+        sum_c0[here].end()
+        x0 = dot3(lower_inv[...], y0[here] - s0[here])
+        head = jnp.where(mine == 0, x0, held_x[here])
+        solution_out[:, parts[here]] = jnp.where(mine >= PANELS, tail[:, parts[here]], head)
+
+    second(0)
+    sum_y0[1].gather()
+    partial(1, c3)
+    sum_y0[1].end()
+    second(1)
+    sum_y1[0].middle()
+    partial(0, c4)
+    sum_y1[0].finish()
+    sum_y1[1].middle()
+    sum_y1[0].gather()
+    sum_y1[1].finish()
+    sum_c2[0].end()
+    sum_c2[1].end()
+    sum_y1[0].end()
+    third(0)
+    sum_y1[1].gather()
+    sum_c1[0].middle()
+    sum_y1[1].end()
+    third(1)
+    sum_c1[0].finish()
+    sum_c1[1].middle()
+    sum_c1[0].gather()
+    sum_y2[0].middle()
+    sum_c1[1].finish()
+    sum_y2[1].middle()
+    sum_c1[0].end()
+    fourth(0)
+    sum_c1[1].gather()
+    sum_y2[0].finish()
+    sum_c0[0].middle()
+    sum_c1[1].end()
+    fourth(1)
+    sum_y2[1].finish()
+    sum_c0[0].finish()
+    sum_c0[1].middle()
+    sum_c0[0].gather()
+    sum_y2[0].gather()
+    sum_c0[1].finish()
+    sum_y2[1].gather()
+    sum_c0[1].gather()
+    forward_end(0)
+    backward_end(0)
+    forward_end(1)
+    backward_end(1)
+    for both in (sum_y0, sum_c2, sum_y1, sum_c1, sum_y2, sum_c0):
+        for one in both:
+            one.drain()
 
 
 def body(row_count, u_panels, u_diag, l_panels, right_side, x_tail, slot_blocks):
@@ -300,10 +354,11 @@
     square, block = (PANEL, PANEL), (PANEL, width)
     outer = row_count // 2
     piece = PANEL // row_count
-    sums = 6
+    sums = 6 * HALVES
+    halves = (HALVES, PANEL, width // HALVES)
     vmem = pl.BlockSpec(memory_space=pltpu.VMEM)
     far = pl.BlockSpec(memory_space=pl.ANY)
-    slots = pltpu.VMEM((sums, outer, piece, width), F32)
+    slots = pltpu.VMEM((sums, outer, piece, width // HALVES), F32)
     return pl.pallas_call(
         chain,
         in_specs=[pl.BlockSpec(memory_space=pltpu.SMEM), far, far, vmem, far, far],
@@ -312,7 +367,7 @@
         scratch_shapes=[pltpu.VMEM((PANELS, *square), F32)] * 2
         + [pltpu.VMEM(block, F32)] * 2
         + [pltpu.VMEM(square, F32)] * 3
-        + [pltpu.VMEM(block, F32)] * 14
+        + [pltpu.VMEM(halves, F32)] * 14
         + [slots] * 3
         + [pltpu.SemaphoreType.DMA((sums, 4, outer))] * 2
         + [pltpu.SemaphoreType.DMA((8,))],

time: 125 us -> 121 us (0.968)
  Pallas kernels: 118 us -> 115 us
    pallas_call x1, Pallas kernels: 118 us -> 115 us  [body(): pl.pallas_call(chain, in_specs=[pl.BlockSpec(memory_space=pltpu.SMEM), fa...]
where the time goes in v4:
time: 121 us
  Pallas kernels  115 us (95%)
  local copies, waits for them, and re-layouts  5.03 us (4%)
    pallas_call x1, Pallas kernels, body(): pl.pallas_call(chain, in_specs=[pl.BlockSpec(memory_space=pltpu.SMEM), fa...  115 us
    unnamed x2, local copies, waits for them, and re-layouts  3.74 us

profile of v4, /device:TPU:0, one launch (start us, length us, event | category | flops | bytes accessed | tf_op | source)
XLA Modules:
  0.0 120.6 jit_solution(15461912812983769706)
XLA Ops:
  0.6 1.3 %reshape.7.diag = f32[1,1536]{1,0:T(1,128)} reshape(f32[1536]{0:T(1024)} %param.7) | data formatting | bytes 12288 | tf_op jit(solution)/shard_map/reshape | solution.py:377
  1.9 115.0 %shard_map.77 = (f32[512,256]{1,0:T(8,128)}, f32[512,256]{1,0:T(8,128)}) custom-call(s32[8]{0:T(128)} %slots.1, f32[512,1536]{1,0:T(8,128)} %upper_far.1, f32[512,1536]{1,0:T(8,128)} %lower_far.1, f32[1,1536]{1,0:T(1,128)} %reshape.7.diag, f32[512,256]{1,0:T(8,128)} %rhs_far.1, f32[512,256]{1,0:T(8,128)} %tail_far.1), custom_call_target="tpu_custom_call" | custom-call | tf_op jit(solution)/shard_map/pallas_call | solution.py:362
  116.9 1.9 %copy.10 = f32[512,256]{1,0:T(8,128)} copy(f32[512,256]{1,0:T(8,128)} %get-tuple-element.4) | data formatting | bytes 1048576
  118.8 1.9 %copy.11 = f32[512,256]{1,0:T(8,128)} copy(f32[512,256]{1,0:T(8,128)} %get-tuple-element.5) | data formatting | bytes 1048576
